TPU v7x, 128 devices: a whole 4x4x4 slice. The times are simulated.
128 devices in a mesh: expert: 8 (over z, y_lo), replica: 16 (over x, y_hi, core).
Axes of the slice: x: 4, y: 4 (y_hi: 2, y_lo: 2; y = y_hi * 2 + y_lo), z: 4, core: 2. Of those that a mesh axis runs over, the one named last changes fastest.
Arguments:
- tokens: bfloat16 [16384, 3584], P(('expert', 'replica')), may hold values from -6 to 6
- routes: int32 [16384, 2], P(('expert', 'replica')), may hold values from 0 to 7, all different within a row; in each aligned block of 128 rows (0 to 127, 128 to 255, ...) at most 64 rows name the same one
- cotangent: bfloat16 [16384, 2, 1280], P(('expert', 'replica')), may hold values from -0.08984375 to 0.08984375
- weights: bfloat16 [8, 3584, 1280], P('expert', 'replica'), may hold values from -0.09375 to 0.09375
- first_moment: float32 [8, 3584, 1280], P('expert', 'replica'), may hold values from -6 to 6
- second_moment: float32 [8, 3584, 1280], P('expert', 'replica'), may hold values from 0.25 to 4
- pairing: int32 [8], replicated, may hold values from 0 to 7, as said below
Outputs:
- activation: bfloat16 [16384, 2, 1280], P(('expert', 'replica'))
- new_weights: bfloat16 [8, 3584, 1280], P('expert', 'replica')
- new_first: float32 [8, 3584, 1280], P('expert', 'replica')
- new_second: float32 [8, 3584, 1280], P('expert', 'replica')
- update: float32 [8, 3584, 1280], P('expert', 'replica')
Inputs may be any that keep to these rules, and one draw needn't show every extreme that they name: `routes`: each row names 2 different experts. Within the rows of one device no expert is named by more than 64 rows, and in every draw some device names some expert in exactly 64 rows. The experts fall into pairs: pairing[pairing[s]] == s and pairing[s] != s for every s.
All inputs are finite; a program needn't handle non-finite values.
Results may differ from a plain program's by a relative error of at most 0.0045.
Values may be sent and summed in bfloat16 or wider, within the bound.
A program may use at most 128 MiB of HBM per device.

v0:
```python
import jax
import jax.numpy as jnp
from jax import lax
from jax.sharding import PartitionSpec as P

BETA_ONE = 0.8
BETA_TWO = 0.9
EPSILON = 1e-08


def relocate_weight(weight_block, pairing):
    slot_count = pairing.shape[0]
    row_total = weight_block.shape[1]
    pieces = weight_block.reshape(slot_count, row_total // slot_count, weight_block.shape[2])
    spread = lax.all_to_all(pieces, "expert", split_axis=0, concat_axis=0, tiled=True)
    chosen = jnp.take(spread, pairing, axis=0)
    settled = lax.all_to_all(chosen, "expert", split_axis=0, concat_axis=0, tiled=True)
    return settled.reshape(weight_block.shape)


def relocate_state(first_block, second_block, pairing):
    slot_count = pairing.shape[0]
    row_total = first_block.shape[1]
    piece_shape = (slot_count, row_total // slot_count, first_block.shape[2])
    first_spread, second_spread = (
        lax.all_to_all(
            first_block.reshape(piece_shape), "expert", split_axis=0, concat_axis=0, tiled=True
        ),
        lax.all_to_all(
            second_block.reshape(piece_shape), "expert", split_axis=0, concat_axis=0, tiled=True
        ),
    )
    first_chosen = jnp.take(first_spread, pairing, axis=0)
    second_chosen = jnp.take(second_spread, pairing, axis=0)
    first_back, second_back = (
        lax.all_to_all(first_chosen, "expert", split_axis=0, concat_axis=0, tiled=True),
        lax.all_to_all(second_chosen, "expert", split_axis=0, concat_axis=0, tiled=True),
    )
    return (first_back.reshape(first_block.shape), second_back.reshape(second_block.shape))


def body(tokens, routes, cotangent, weights, first_moment, second_moment, pairing):
    slot_count = pairing.shape[0]
    tok_rows, choose_count = routes.shape
    hidden_width = cotangent.shape[2]
    model_width = tokens.shape[1]
    capacity = 2 * tok_rows * choose_count // slot_count
    flat_routes = routes.reshape(-1)
    one_hot = (flat_routes[:, None] == jnp.arange(slot_count, dtype=jnp.int32)[None, :]).astype(
        jnp.int32
    )
    places = jnp.sum((jnp.cumsum(one_hot, axis=0) - 1) * one_hot, axis=1)
    weights = relocate_weight(weights, pairing)
    first_moment, second_moment = relocate_state(first_moment, second_moment, pairing)
    owners = jnp.take(pairing, flat_routes)
    targets = owners * capacity + places
    sources = jnp.arange(tok_rows * choose_count, dtype=jnp.int32) // choose_count
    sent_rows = (
        jnp.zeros((slot_count * capacity, model_width), jnp.bfloat16)
        .at[targets]
        .set(tokens[sources])
    )
    sent_grads = (
        jnp.zeros((slot_count * capacity, hidden_width), jnp.bfloat16)
        .at[targets]
        .set(cotangent.reshape(-1, hidden_width))
    )
    came_rows, came_grads = (
        lax.all_to_all(
            sent_rows.reshape(slot_count, capacity, model_width),
            "expert",
            split_axis=0,
            concat_axis=0,
            tiled=True,
        ),
        lax.all_to_all(
            sent_grads.reshape(slot_count, capacity, hidden_width),
            "expert",
            split_axis=0,
            concat_axis=0,
            tiled=True,
        ),
    )
    came_rows = came_rows.reshape(slot_count * capacity, model_width)
    came_grads = came_grads.reshape(slot_count * capacity, hidden_width)
    weight_shard = weights.reshape(weights.shape[1], hidden_width)
    projected = jnp.dot(
        came_rows,
        lax.all_gather(weight_shard, "replica", axis=0, tiled=True),
        preferred_element_type=jnp.float32,
    ).astype(jnp.bfloat16)
    returned = lax.all_to_all(
        projected.reshape(slot_count, capacity, hidden_width),
        "expert",
        split_axis=0,
        concat_axis=0,
        tiled=True,
    )
    activation = returned.reshape(slot_count * capacity, hidden_width)[targets].reshape(
        tok_rows, choose_count, hidden_width
    )
    share_rows = model_width // lax.axis_size("replica")
    partial_value = lax.dot_general(
        came_rows, came_grads, (((0,), (0,)), ((), ())), preferred_element_type=jnp.float32
    )
    summed = lax.psum(partial_value.astype(jnp.bfloat16), "replica").astype(jnp.float32)
    gradient = lax.dynamic_slice_in_dim(
        summed, lax.axis_index("replica") * share_rows, share_rows, 0
    )
    gradient = gradient.reshape(first_moment.shape)
    new_first = BETA_ONE * first_moment + (1.0 - BETA_ONE) * gradient
    new_second = BETA_TWO * second_moment + (1.0 - BETA_TWO) * gradient * gradient
    update = new_first / (jnp.sqrt(new_second) + EPSILON)
    return (activation, weights, new_first, new_second, update)


def solution(mesh):
    in_specs = (
        P(("expert", "replica"), None),
        P(("expert", "replica"), None),
        P(("expert", "replica"), None, None),
        P("expert", "replica", None),
        P("expert", "replica", None),
        P("expert", "replica", None),
        P(),
    )
    out_specs = (
        P(("expert", "replica"), None, None),
        P("expert", "replica", None),
        P("expert", "replica", None),
        P("expert", "replica", None),
        P("expert", "replica", None),
    )
    return jax.shard_map(body, mesh=mesh, in_specs=in_specs, out_specs=out_specs, check_vma=False)
```

profile of v0, /device:TPU:1, one launch (start us, length us, event | category | flops | bytes accessed | tf_op | source)
XLA Modules:
  0.0 440.6 jit_solution(7737302614544001890)
XLA Ops:
  7.2 2.1 reshape.221
  9.3 6.9 %all-to-all-start.1 = ((bf16[8,28,1280]{2,1,0:T(8,128)(2,1)}), bf16[8,28,1280]{2,1,0:T(8,128)(2,1)S(1)}, u32[]{:S(2)}, u32[]{:S(2)}) async-start(bf16[8,28,1280]{2,1,0:T(8,128)(2,1)} %reshape.221), calls=%async_computation.1 | async-start | bytes 1310720 | tf_op jit(solution)/shard_map/all_to_all | solution.py:15
  16.3 10.2 %all-to-all-done.1 = bf16[8,28,1280]{2,1,0:T(8,128)(2,1)S(1)} async-done(((bf16[8,28,1280]{2,1,0:T(8,128)(2,1)}), bf16[8,28,1280]{2,1,0:T(8,128)(2,1)S(1)}, u32[]{:S(2)}, u32[]{:S(2)}) %all-to-all-start.1) | async-done | bytes 573472 | tf_op jit(solution)/shard_map/all_to_all | solution.py:15
  26.5 0.6 gather_fusion
  27.1 0.1 broadcast_select_fusion.2
  27.2 13.6 %all_to_all.45 = bf16[8,28,1280]{2,1,0:T(8,128)(2,1)S(1)} all-to-all(bf16[8,28,1280]{2,1,0:T(8,128)(2,1)S(1)} %broadcast_select_fusion.2), channel_id=1, replica_groups=mesh['expert'=8,'replica'=16] {'expert'}, dimensions={0} | all-to-all | bytes 1146880 | tf_op jit(solution)/shard_map/all_to_all | solution.py:17
  40.8 0.9 reshape_reshape.3
  41.9 0.1 eq.29
  42.0 0.1 eq.25
  42.2 0.1 reshape.217
  42.3 0.6 reduce-window.6
  42.9 0.2 slice_reduce_fusion
  43.2 0.3 reshape.297
  43.5 0.7 fusion.11
  44.2 4.5 %compare_select_fusion.3 = s32[256,1]{0,1:T(1,128)S(1)} fusion(s32[]{:T(128)} %bitcast.1, s32[]{:T(128)} %bitcast.2, s32[]{:T(128)} %bitcast.3, s32[]{:T(128)} %bitcast.4, s32[]{:T(128)} %bitcast.5, s32[]{:T(128)} %bitcast.7, s32[]{:T(128)} %bitcast.6, s32[256,1]{0,1:T(1,128)S(1)} %reshape.217), kind=kLoop, calls=%fused_computation.39 | loop fusion | flops 3840 | bytes 2076 | tf_op jit(solution)/shard_map/jit(_take)/gather | solution.py:55
  48.7 0.7 broadcast_select_fusion.3
  49.4 2.9 scatter_custom_fusion.1
  52.4 3.6 all-to-all-start.6
  55.9 0.2 all-reduce.2.cloned.1.call-start
  56.2 10.9 %scatter_custom_fusion = bf16[512,3584]{1,0:T(8,128)(2,1)} fusion(s32[256]{0:T(256)S(1)} %bitcast.40, bf16[128,3584]{1,0:T(8,128)(2,1)S(1)} %copy-done, s32[1024]{0:T(1024)S(1)} %pad_clamp_fusion.2, bf16[]{:T(256)} %constant.44.clone.1), kind=kCustom, calls=%fused_computation.9 | custom fusion | bytes 3670018 | tf_op jit(solution)/shard_map/scatter | solution.py:61
  67.1 10.7 %all-to-all-done.6 = bf16[8,64,1280]{2,1,0:T(8,128)(2,1)S(1)} async-done(((bf16[8,64,1280]{2,1,0:T(8,128)(2,1)}), bf16[8,64,1280]{2,1,0:T(8,128)(2,1)S(1)}, u32[]{:S(2)}, u32[]{:S(2)}) %all-to-all-start.6) | async-done | bytes 1310752 | tf_op jit(solution)/shard_map/all_to_all | solution.py:76
  77.8 69.3 %all_to_all.46 = bf16[8,64,3584]{2,1,0:T(8,128)(2,1)S(1)} all-to-all(bf16[8,64,3584]{2,1,0:T(8,128)(2,1)} %bitcast.37), channel_id=1, replica_groups=mesh['expert'=8,'replica'=16] {'expert'}, dimensions={0} | all-to-all | bytes 7340032 | tf_op jit(solution)/shard_map/all_to_all | solution.py:69
  147.1 1.9 copy-done.3
  149.0 7.4 %bitcast_convert_fusion = bf16[3584,1280]{1,0:T(8,128)(2,1)} fusion(bf16[8,64,3584]{2,1,0:T(8,128)(2,1)S(1)} %all_to_all.46, bf16[8,64,1280]{2,1,0:T(8,128)(2,1)S(1)} %all-to-all-done.6), kind=kOutput, calls=%fused_computation.7 | convolution fusion | flops 4702208000 | bytes 14155776 | tf_op jit(solution)/shard_map/dot_general | solution.py:103
  156.4 1.2 copy-done.4
  157.7 1.2 reshape.229
  158.8 3.6 all-to-all-start.7
  162.4 2.4 reshape.226
  164.9 29.6 %all-to-all-done.7 = f32[8,28,1280]{2,1,0:T(8,128)S(1)} async-done(((f32[8,28,1280]{2,1,0:T(8,128)}), f32[8,28,1280]{2,1,0:T(8,128)S(1)}, u32[]{:S(2)}, u32[]{:S(2)}) %all-to-all-start.7) | async-done | bytes 1146912 | tf_op jit(solution)/shard_map/all_to_all | solution.py:29
  194.4 4.3 all-to-all-start.4
  198.7 1.7 gather_fusion.3
  200.4 32.0 %all-to-all-done.4 = f32[8,28,1280]{2,1,0:T(8,128)} async-done(((f32[8,28,1280]{2,1,0:T(8,128)}), f32[8,28,1280]{2,1,0:T(8,128)}, u32[]{:S(2)}, u32[]{:S(2)}) %all-to-all-start.4) | async-done | bytes 1146912 | tf_op jit(solution)/shard_map/all_to_all | solution.py:26
  232.4 3.0 gather_fusion.2
  235.4 3.1 broadcast_select_fusion
  238.6 3.6 all-to-all-start.5
  242.1 0.9 reshape.225
  243.1 34.7 %all-to-all-done.5 = f32[8,28,1280]{2,1,0:T(8,128)S(1)} async-done(((f32[8,28,1280]{2,1,0:T(8,128)}), f32[8,28,1280]{2,1,0:T(8,128)S(1)}, u32[]{:S(2)}, u32[]{:S(2)}) %all-to-all-start.5) | async-done | bytes 1146912 | tf_op jit(solution)/shard_map/all_to_all | solution.py:36
  277.8 4.3 all-to-all-start.8
  282.2 1.1 mul.62
  283.3 10.7 %convolution_convert_fusion = bf16[512,1280]{1,0:T(8,128)(2,1)} fusion(bf16[512,3584]{1,0:T(8,128)(2,1)} %bitcast.38, bf16[3584,1280]{1,0:T(8,128)(2,1)} %all-gather.2.cloned.1.call-done), kind=kOutput, calls=%fused_computation.8 | convolution fusion | flops 4698275840 | bytes 14155776 | tf_op jit(solution)/shard_map/dot_general | solution.py:87
  294.1 20.6 %all-to-all-done.8 = f32[8,28,1280]{2,1,0:T(8,128)} async-done(((f32[8,28,1280]{2,1,0:T(8,128)}), f32[8,28,1280]{2,1,0:T(8,128)}, u32[]{:S(2)}, u32[]{:S(2)}) %all-to-all-start.8) | async-done | bytes 1146912 | tf_op jit(solution)/shard_map/all_to_all | solution.py:37
  314.6 3.6 all-to-all-start.3
  318.2 1.4 broadcast_multiply_fusion
  319.7 1.1 mul.68
  320.8 106.9 %all-reduce.2.cloned.1.call-done = bf16[3584,1280]{1,0:T(8,128)(2,1)} async-done(((bf16[3584,1280]{1,0:T(8,128)(2,1)}), bf16[3584,1280]{1,0:T(8,128)(2,1)}) %all-reduce.2.cloned.1.call-update) | async-done | bytes 9175056 | tf_op jit(solution)/shard_map/psum | solution.py:106
  427.6 3.8 divide_bitcast_fusion
  431.4 1.3 gather_fusion.1
  432.7 1.1 reshape.224
  (33 shorter events, 0.6 us)
Async XLA Ops:
  7.2 49.0 %copy-start = (bf16[128,3584]{1,0:T(8,128)(2,1)S(1)}, bf16[128,3584]{1,0:T(8,128)(2,1)}, u32[]{:S(2)}) copy-start(bf16[128,3584]{1,0:T(8,128)(2,1)} %param.9) | copy-start | bytes 2752516
  7.2 9.0 %copy-start.6 = (s32[8]{0:T(128)S(1)}, s32[8]{0:T(128)}, u32[]{:S(2)}) copy-start(s32[8]{0:T(128)} %param.15) | copy-start | bytes 100
  9.3 17.2 %all-to-all-start.1 = ((bf16[8,28,1280]{2,1,0:T(8,128)(2,1)}), bf16[8,28,1280]{2,1,0:T(8,128)(2,1)S(1)}, u32[]{:S(2)}, u32[]{:S(2)}) async-start(bf16[8,28,1280]{2,1,0:T(8,128)(2,1)} %reshape.221), calls=%async_computation.1 | async-start | bytes 1310720 | tf_op jit(solution)/shard_map/all_to_all | solution.py:15
  16.2 267.2 %all-gather.2.cloned.1.call-start = ((), (), s32[]{:S(2)}) async-start(), calls=%async_computation.9 | async-start | bytes 9748480 | tf_op jit(solution)/shard_map/all_gather | solution.py:89
  27.2 14.6 %copy-start.7 = (s32[128,2]{0,1:T(2,128)S(1)}, s32[128,2]{0,1:T(2,128)}, u32[]{:S(2)}) copy-start(s32[128,2]{0,1:T(2,128)} %param.10) | copy-start | bytes 3076
  40.8 2.4 copy-start.5
  52.4 25.4 %all-to-all-start.6 = ((bf16[8,64,1280]{2,1,0:T(8,128)(2,1)}), bf16[8,64,1280]{2,1,0:T(8,128)(2,1)S(1)}, u32[]{:S(2)}, u32[]{:S(2)}) async-start(bf16[8,64,1280]{2,1,0:T(8,128)(2,1)} %bitcast.19), calls=%async_computation.6 | async-start | bytes 2621440 | tf_op jit(solution)/shard_map/all_to_all | solution.py:76
  55.9 371.7 %all-reduce.2.cloned.1.call-start = ((), (), s32[]{:S(2)}) async-start(), calls=%async_computation.10 | async-start | bytes 18350080 | tf_op jit(solution)/shard_map/psum | solution.py:106
  147.1 1.9 copy-start.3
  156.4 1.3 copy-start.4
  158.8 35.6 %all-to-all-start.7 = ((f32[8,28,1280]{2,1,0:T(8,128)}), f32[8,28,1280]{2,1,0:T(8,128)S(1)}, u32[]{:S(2)}, u32[]{:S(2)}) async-start(f32[8,28,1280]{2,1,0:T(8,128)} %reshape.229), calls=%async_computation.7 | async-start | bytes 2621440 | tf_op jit(solution)/shard_map/all_to_all | solution.py:29
  194.4 38.0 %all-to-all-start.4 = ((f32[8,28,1280]{2,1,0:T(8,128)}), f32[8,28,1280]{2,1,0:T(8,128)}, u32[]{:S(2)}, u32[]{:S(2)}) async-start(f32[8,28,1280]{2,1,0:T(8,128)} %reshape.226), calls=%async_computation.4 | async-start | bytes 2621440 | tf_op jit(solution)/shard_map/all_to_all | solution.py:26
  200.4 35.0 %copy-start.2 = (f32[8,28,1280]{2,1,0:T(8,128)S(1)}, f32[8,28,1280]{2,1,0:T(8,128)}, u32[]{:S(2)}) copy-start(f32[8,28,1280]{2,1,0:T(8,128)} %gather_fusion.3) | copy-start | bytes 3440644
  238.6 39.2 %all-to-all-start.5 = ((f32[8,28,1280]{2,1,0:T(8,128)}), f32[8,28,1280]{2,1,0:T(8,128)S(1)}, u32[]{:S(2)}, u32[]{:S(2)}) async-start(f32[8,28,1280]{2,1,0:T(8,128)} %get-tuple-element.10), calls=%async_computation.5 | async-start | bytes 2621440 | tf_op jit(solution)/shard_map/all_to_all | solution.py:36
  277.8 36.8 %all-to-all-start.8 = ((f32[8,28,1280]{2,1,0:T(8,128)}), f32[8,28,1280]{2,1,0:T(8,128)}, u32[]{:S(2)}, u32[]{:S(2)}) async-start(f32[8,28,1280]{2,1,0:T(8,128)} %get-tuple-element.9), calls=%async_computation.8 | async-start | bytes 2621440 | tf_op jit(solution)/shard_map/all_to_all | solution.py:37
  314.6 116.8 %all-to-all-start.3 = ((bf16[8,64,1280]{2,1,0:T(8,128)(2,1)}), bf16[8,64,1280]{2,1,0:T(8,128)(2,1)S(1)}, u32[]{:S(2)}, u32[]{:S(2)}) async-start(bf16[8,64,1280]{2,1,0:T(8,128)(2,1)} %bitcast.17), calls=%async_computation.3 | async-start | bytes 2621440 | tf_op jit(solution)/shard_map/all_to_all | solution.py:92
  431.4 2.3 copy-start.1
Sparse Core Ops, SparseCore 0:
  41.9 100.2 all-gather.1
  156.5 271.0 all-reduce.1
where the time goes:
time: 442 us; the launch traced here: 441 us
  waiting for transfers between devices  245 us (55%)
  blocking collectives  83 us (19%)
  local copies, waits for them, and re-layouts  36.1 us (8%)
  starting transfers between devices  29.9 us (7%)
  matrix products  18.1 us (4%)
  other arithmetic  14.5 us (3%)
  between operations  14.3 us (3%)
    psum x1, waiting for transfers between devices, body(): lax.psum(partial_value.astype(jnp.bfloat16), 'replica').astype(jnp.float32)  107 us
    all_to_all x1, blocking collectives, body(): lax.all_to_all(sent_rows.reshape(slot_count, capacity, model_width), 'exp...  69.3 us
    all_to_all x1, waiting for transfers between devices, relocate_state(): lax.all_to_all(first_chosen, 'expert', split_axis=0, concat_axis=0, tiled...  34.7 us
    all_to_all x1, waiting for transfers between devices, relocate_state(): lax.all_to_all(first_block.reshape(piece_shape), 'expert', split_axis=0,...  32 us
    all_to_all x1, waiting for transfers between devices, relocate_state(): lax.all_to_all(second_block.reshape(piece_shape), 'expert', split_axis=0,...  29.6 us
    all_to_all x1, waiting for transfers between devices, relocate_state(): lax.all_to_all(second_chosen, 'expert', split_axis=0, concat_axis=0, tile...  20.6 us
    all_to_all x1, blocking collectives, relocate_weight(): lax.all_to_all(chosen, 'expert', split_axis=0, concat_axis=0, tiled=True)  13.6 us
    scatter x1, local copies, waits for them, and re-layouts, body(): sent_rows = jnp.zeros((slot_count * capacity, model_width), jnp.bfloat16)...  10.9 us
  transfers between devices with their start and end apart: 9, of which 7 were waited for; matrix products, arithmetic and copies ran while one was open for 14% of the time, Pallas kernels for 0%

commit v1 on v0

v1 whole, which is shorter than its diff:
```python
import jax
import jax.numpy as jnp
from jax import lax
from jax.experimental import pallas as pl
from jax.experimental.pallas import tpu as pltpu
from jax.sharding import PartitionSpec as P

BETA_ONE = 0.8
BETA_TWO = 0.9
EPSILON = 1e-08
MESH = pl.DeviceIdType.MESH
BF = jnp.bfloat16
F32 = jnp.float32

D, FW, TOK, CAP, NE, SHARD, CHUNK = 3584, 1280, 128, 64, 8, 224, 896
ROWS = NE * CAP
TILE = 256


def kernel(
    pair, rt, tok, cot, w, m1, m2,
    act, wn, m1n, m2n, g,
    w1, w2s, wfull, b1s, b1r, b2s, b2r, tp, tr, cp, cr, acc, ps, pr, part, sibr, xr, yr, g0, g1,
    s_m, s_w1, r_w1, s_w2, r_w2, s_b1, r_b1, s_b2, r_b2, s_t, r_t, s_c, r_c, s_e, r_e,
    s_ag, r_ag, s_sb, r_sb, s_x, r_x, s_y, r_y,
):
    e = lax.axis_index("expert")
    r = lax.axis_index("replica")
    x = r // 4
    yh = (r // 2) % 2
    c = r % 2

    def rid(x_, yh_, c_):
        return x_ * 4 + yh_ * 2 + c_

    xp, xm, xo = (x + 1) % 4, (x + 3) % 4, (x + 2) % 4
    sib = (e, rid(x, yh, 1 - c))
    yp = (e, rid(x, 1 - yh, c))
    px = (e, rid(xp, yh, c))
    mx = (e, rid(xm, yh, c))

    def rc(src, dst, ss, rs, dev):
        return pltpu.make_async_remote_copy(
            src_ref=src, dst_ref=dst, send_sem=ss, recv_sem=rs, device_id=dev, device_id_type=MESH
        )

    def got(ref, sem):
        rc(ref, ref, sem, sem, sib).wait_recv()

    def gone(ref, sem):
        rc(ref, ref, sem, sem, sib).wait_send()

    loads = [
        pltpu.make_async_copy(m1, acc.at[pl.ds(0, SHARD)], s_m.at[0]),
        pltpu.make_async_copy(m2, acc.at[pl.ds(SHARD, SHARD)], s_m.at[1]),
    ]
    for load in loads:
        load.start()

    barrier = pltpu.get_barrier_semaphore()

    @pl.loop(1, NE)
    def _(d):
        pl.semaphore_signal(barrier, inc=1, device_id=((e + d) % NE, r), device_id_type=MESH)

    for dev in (sib, yp, px, mx):
        pl.semaphore_signal(barrier, inc=1, device_id=dev, device_id_type=MESH)
    pl.semaphore_wait(barrier, NE - 1 + 4)

    @pl.loop(0, 7)
    def _(i):
        rows = pl.ds(pl.multiple_of(i * 32, 32), 32)

        @pl.when(i != e)
        def _():
            rc(w.at[rows], w1.at[e], s_w1.at[i], r_w1.at[e], (i, r)).start()

        @pl.when(i == e)
        def _():
            w1[e] = w[rows, :]

    owners = []
    for k in range(2):
        row = rt[k : k + 1, :]
        own = jnp.zeros_like(row)
        for s in range(NE):
            own = own + jnp.where(row == s, pair[s], 0)
        owners.append(own)
    places = lax.broadcasted_iota(jnp.int32, (NE, TOK), 0)
    named = [(places == own) for own in owners]
    mask = jnp.where(named[0] | named[1], 1.0, 0.0)
    earlier = jnp.where(
        lax.broadcasted_iota(jnp.int32, (TOK, TOK), 0) < lax.broadcasted_iota(jnp.int32, (TOK, TOK), 1), 1.0, 0.0
    )
    rank = jnp.dot(mask.astype(BF), earlier.astype(BF), preferred_element_type=F32)
    slots = lax.broadcasted_iota(jnp.int32, (ROWS, TOK), 0).astype(F32)
    for k, ref in ((0, g0), (1, g1)):
        slot = jnp.sum(jnp.where(named[k], rank, 0.0), axis=0, keepdims=True) + owners[k].astype(F32) * CAP
        ref[...] = jnp.where(slots == slot, 1.0, 0.0).astype(BF)

    @pl.loop(0, FW // TILE)
    def _(n):
        a = jnp.dot(g0[...], cot[:, pl.ds(pl.multiple_of(n * TILE, TILE), TILE)], preferred_element_type=F32)
        b = jnp.dot(g1[...], cot[:, pl.ds(pl.multiple_of(FW + n * TILE, TILE), TILE)], preferred_element_type=F32)
        cp[:, :, pl.ds(pl.multiple_of(n * TILE, TILE), TILE)] = (a + b).astype(BF).reshape(NE, CAP, TILE)

    @pl.when(e < 7)
    def _():
        @pl.loop(0, NE)
        def _(s):
            @pl.when(s != e)
            def _():
                got(w1.at[s], r_w1.at[s])

        rows = pl.ds(pl.multiple_of(e * 32, 32), 32)

        @pl.loop(0, NE)
        def _(s):
            v = w1[pair[s]]
            w2s[s] = v

            @pl.when(s != e)
            def _():
                rc(w2s.at[s], wfull.at[r, rows], s_w2.at[s], r_w2.at[e], (s, r)).start()

            @pl.when(s == e)
            def _():
                wfull[r, rows, :] = v

    def spread(src, dst, ss, rs):
        @pl.loop(1, NE)
        def _(d):
            s = (e + d) % NE
            rc(src(s), dst(e), ss(s), rs(e), (s, r)).start()

    spread(lambda s: cp.at[s], lambda s: cr.at[s], lambda s: s_c.at[s], lambda s: r_c.at[s])
    cr[e] = cp[e]

    order = (xo, xp, xm, x)
    for q in order[:2]:
        send_chunk(q, e, r, tok, g0, g1, tp, tr, s_t, r_t, spread)

    @pl.loop(0, 7)
    def _(i):
        @pl.when(i != e)
        def _():
            got(wfull.at[r, pl.ds(pl.multiple_of(i * 32, 32), 32)], r_w2.at[i])

    def ag(shard, k, dev):
        rc(wfull.at[shard], wfull.at[shard], s_ag.at[k], r_ag.at[shard], dev).start()

    ag(r, 0, yp)
    ag(r, 1, px)
    ag(r, 2, mx)
    ag(r, 3, sib)

    for q in order[2:]:
        send_chunk(q, e, r, tok, g0, g1, tp, tr, s_t, r_t, spread)

    for load in loads:
        load.wait()

    @pl.loop(0, NE)
    def _(p):
        rows = pl.ds(pl.multiple_of((p // 4) * SHARD + ((p // 2) % 2) * 112, 8), 112)
        cols = pl.ds(pl.multiple_of((p % 2) * 640, 128), 640)
        b1s[p] = acc[rows, cols].astype(BF)

        @pl.when(p != e)
        def _():
            rc(b1s.at[p], b1r.at[e], s_b1.at[p], r_b1.at[e], (p, r)).start()

        @pl.when(p == e)
        def _():
            b1r[e] = b1s[p]

    wn[...] = wfull[r]

    @pl.loop(1, NE)
    def _(d):
        s = (e + d) % NE
        got(cr.at[s], r_c.at[s])

    def wgrad(q):
        @pl.loop(1, NE)
        def _(d):
            s = (e + d) % NE
            got(tr.at[q, s], r_t.at[q, s])

        @pl.loop(0, FW // TILE)
        def _(n):
            cols = pl.ds(pl.multiple_of(n * TILE, TILE), TILE)
            v = lax.dot_general(
                tr[q].reshape(ROWS, CHUNK), cr[:, :, cols].reshape(ROWS, TILE), (((0,), (0,)), ((), ())),
                preferred_element_type=F32,
            )
            part[pl.ds(q * 4, 4), :, cols] = v.astype(BF).reshape(4, SHARD, TILE)

    def add(shard, other):
        @pl.loop(0, 7)
        def _(i):
            rows = pl.ds(pl.multiple_of(i * 32, 32), 32)
            part[shard, rows, :] = (part[shard, rows, :].astype(F32) + other[rows, :].astype(F32)).astype(BF)

    def to_sib(k, q):
        for h in range(2):
            rc(part.at[rid(q, h, 1 - c)], sibr.at[2 * k + h], s_sb.at[2 * k + h], r_sb.at[2 * k + h], sib).start()

    def from_sib(k, q):
        for h in range(2):
            got(sibr.at[2 * k + h], r_sb.at[2 * k + h])
            add(rid(q, h, c), sibr.at[2 * k + h])

    def xs(shard, slot, dev):
        rc(part.at[shard], xr.at[slot], s_x.at[slot], r_x.at[slot], dev).start()

    wgrad(xo)
    to_sib(0, xo)
    from_sib(0, xo)
    xs(rid(xo, 0, c), 0, px)
    xs(rid(xo, 1, c), 1, mx)

    def from_x(h, k):
        low, high = rid(xm, h, c), rid(xp, h, c)
        got(wfull.at[low], r_ag.at[low])
        ag(low, k, sib)
        got(wfull.at[high], r_ag.at[high])
        ag(high, k + 1, sib)
        ag(rid((x + 3 + 2 * h) % 4, h, c), k + 2, (e, rid((x + 1 + 2 * h) % 4, yh, c)))

    partner = rid(x, 1 - yh, c)
    got(wfull.at[partner], r_ag.at[partner])
    ag(partner, 4, px)
    ag(partner, 5, mx)
    ag(partner, 6, sib)
    from_x(yh, 7)

    wgrad(xp)
    to_sib(1, xp)
    from_sib(1, xp)
    xs(rid(xp, 1, c), 3, px)
    got(xr.at[0], r_x.at[0])
    add(rid(xp, 0, c), xr.at[0])
    xs(rid(xp, 0, c), 2, px)

    wgrad(xm)
    to_sib(2, xm)
    from_sib(2, xm)
    xs(rid(xm, 0, c), 5, mx)
    got(xr.at[1], r_x.at[1])
    add(rid(xm, 1, c), xr.at[1])
    xs(rid(xm, 1, c), 4, mx)

    @pl.loop(1, NE)
    def _(d):
        s = (e + d) % NE
        got(b1r.at[s], r_b1.at[s])

    @pl.loop(0, NE)
    def _(s):
        v = b1r[pair[s]]
        b2s[s] = v

        @pl.when(s != e)
        def _():
            rc(b2s.at[s], b2r.at[e], s_b2.at[s], r_b2.at[e], (s, r)).start()

        @pl.when(s == e)
        def _():
            b2r[e] = v

    from_x(1 - yh, 10)

    wgrad(x)
    to_sib(3, x)
    from_sib(3, x)

    def project(q, first):
        @pl.loop(0, FW // TILE)
        def _(n):
            cols = pl.ds(pl.multiple_of(n * TILE, TILE), TILE)
            v = jnp.dot(
                tr[q].reshape(ROWS, CHUNK), wfull[pl.ds(q * 4, 4), :, cols].reshape(CHUNK, TILE),
                preferred_element_type=F32,
            )
            if first:
                acc[:, cols] = v
            else:
                acc[:, cols] += v

    def sib_has(q):
        for h in range(2):
            shard = rid(q, h, 1 - c)
            got(wfull.at[shard], r_ag.at[shard])

    sib_has(x)
    project(x, True)
    sib_has(xp)
    project(xp, False)
    sib_has(xm)
    project(xm, False)
    far = (rid(xo, yh, c), rid(xo, 1 - yh, c))
    for k in range(2):
        got(wfull.at[far[k]], r_ag.at[far[k]])
        ag(far[k], 13 + k, sib)
    sib_has(xo)
    project(xo, False)

    @pl.loop(0, NE)
    def _(s):
        ps[s] = acc[pl.ds(pl.multiple_of(s * CAP, CAP), CAP), :].astype(BF)

        @pl.when(s != e)
        def _():
            rc(ps.at[s], pr.at[e], s_e.at[s], r_e.at[e], (s, r)).start()

        @pl.when(s == e)
        def _():
            pr[e] = ps[s]

    for k in range(2, 6):
        got(xr.at[k], r_x.at[k])

    def total(h, put):
        @pl.loop(0, 7)
        def _(i):
            rows = pl.ds(pl.multiple_of(i * 32, 32), 32)
            put(
                rows,
                part[rid(x, h, c), rows, :].astype(F32)
                + xr[2 + h, rows, :].astype(F32)
                + xr[5 - h, rows, :].astype(F32),
            )

    def put_part(rows, v):
        part[rid(x, 1 - yh, c), rows, :] = v.astype(BF)

    def put_g(rows, v):
        g[rows, :] = v

    total(1 - yh, put_part)
    ysend = rc(part.at[rid(x, 1 - yh, c)], yr, s_y.at[0], r_y.at[0], yp)
    ysend.start()
    total(yh, put_g)

    @pl.loop(1, NE)
    def _(d):
        s = (e + d) % NE
        got(b2r.at[s], r_b2.at[s])

    for i in range(NE):
        out = m1n if i < 4 else m2n
        a, b = (i // 2) % 2, i % 2
        out[112 * a : 112 * a + 112, 640 * b : 640 * b + 640] = b2r[i]

    @pl.loop(1, NE)
    def _(d):
        s = (e + d) % NE
        got(pr.at[s], r_e.at[s])

    @pl.loop(0, FW // TILE)
    def _(n):
        cols = pl.ds(pl.multiple_of(n * TILE, TILE), TILE)
        for k, ref in ((0, g0), (1, g1)):
            v = lax.dot_general(
                ref[...], pr[:, :, cols].reshape(ROWS, TILE), (((0,), (0,)), ((), ())), preferred_element_type=F32
            )
            act[:, pl.ds(pl.multiple_of(k * FW + n * TILE, TILE), TILE)] = v.astype(BF)

    ysend.wait_recv()

    @pl.loop(0, 7)
    def _(i):
        rows = pl.ds(pl.multiple_of(i * 32, 32), 32)
        g[rows, :] += yr[rows, :].astype(F32)

    ysend.wait_send()
    for k in range(15):
        gone(wfull.at[0], s_ag.at[k])

    @pl.loop(0, 7)
    def _(i):
        @pl.when(i != e)
        def _():
            gone(w1.at[0], s_w1.at[i])

    @pl.loop(0, NE)
    def _(s):
        gone(sibr.at[0], s_sb.at[s])

    @pl.loop(0, 6)
    def _(s):
        gone(xr.at[0], s_x.at[s])

    @pl.loop(1, NE)
    def _(d):
        s = (e + d) % NE

        @pl.when(e < 7)
        def _():
            gone(w2s.at[0], s_w2.at[s])

        gone(b1s.at[0], s_b1.at[s])
        gone(b2s.at[0], s_b2.at[s])
        gone(cp.at[0], s_c.at[s])
        gone(ps.at[0], s_e.at[s])
        for q in range(4):
            gone(tp.at[0, 0], s_t.at[q, s])


def send_chunk(q, e, r, tok, g0, g1, tp, tr, s_t, r_t, spread):
    cols = pl.ds(pl.multiple_of(q * CHUNK, 128), CHUNK)
    v = jnp.dot(g0[...] + g1[...], tok[:, cols], preferred_element_type=F32)
    tp[q] = v.astype(BF).reshape(NE, CAP, CHUNK)
    spread(lambda s: tp.at[q, s], lambda s: tr.at[q, s], lambda s: s_t.at[q, s], lambda s: r_t.at[q, s])
    tr[q, e] = tp[q, e]


def body(tokens, routes, cotangent, weights, first_moment, second_moment, pairing):
    dma = pltpu.SemaphoreType.DMA
    vmem = pl.BlockSpec(memory_space=pltpu.VMEM)
    hbm = pl.BlockSpec(memory_space=pl.ANY)
    act, wn, m1n, m2n, g = pl.pallas_call(
        kernel,
        out_shape=(
            jax.ShapeDtypeStruct((TOK, 2 * FW), BF),
            jax.ShapeDtypeStruct((SHARD, FW), BF),
            jax.ShapeDtypeStruct((SHARD, FW), BF),
            jax.ShapeDtypeStruct((SHARD, FW), BF),
            jax.ShapeDtypeStruct((SHARD, FW), F32),
        ),
        in_specs=[pl.BlockSpec(memory_space=pltpu.SMEM), vmem, vmem, vmem, vmem, hbm, hbm],
        out_specs=(vmem,) * 5,
        scratch_shapes=[
            pltpu.VMEM((NE, 32, FW), BF),
            pltpu.VMEM((NE, 32, FW), BF),
            pltpu.VMEM((16, SHARD, FW), BF),
            pltpu.VMEM((NE, 112, 640), BF),
            pltpu.VMEM((NE, 112, 640), BF),
            pltpu.VMEM((NE, 112, 640), BF),
            pltpu.VMEM((NE, 112, 640), BF),
            pltpu.VMEM((4, NE, CAP, CHUNK), BF),
            pltpu.VMEM((4, NE, CAP, CHUNK), BF),
            pltpu.VMEM((NE, CAP, FW), BF),
            pltpu.VMEM((NE, CAP, FW), BF),
            pltpu.VMEM((ROWS, FW), F32),
            pltpu.VMEM((NE, CAP, FW), BF),
            pltpu.VMEM((NE, CAP, FW), BF),
            pltpu.VMEM((16, SHARD, FW), BF),
            pltpu.VMEM((NE, SHARD, FW), BF),
            pltpu.VMEM((6, SHARD, FW), BF),
            pltpu.VMEM((SHARD, FW), BF),
            pltpu.VMEM((ROWS, TOK), BF),
            pltpu.VMEM((ROWS, TOK), BF),
            dma((2,)),
            dma((NE,)), dma((NE,)), dma((NE,)), dma((NE,)),
            dma((NE,)), dma((NE,)), dma((NE,)), dma((NE,)),
            dma((4, NE)), dma((4, NE)),
            dma((NE,)), dma((NE,)), dma((NE,)), dma((NE,)),
            dma((15,)), dma((16,)),
            dma((NE,)), dma((NE,)),
            dma((6,)), dma((6,)),
            dma((1,)), dma((1,)),
        ],
        compiler_params=pltpu.CompilerParams(
            collective_id=0, has_side_effects=True, vmem_limit_bytes=63 * 1024 * 1024
        ),
    )(
        pairing,
        routes.T,
        tokens,
        cotangent.reshape(TOK, 2 * FW),
        weights.reshape(SHARD, FW),
        first_moment.reshape(SHARD, FW),
        second_moment.reshape(SHARD, FW),
    )
    new_first = BETA_ONE * m1n.astype(F32) + (1.0 - BETA_ONE) * g
    new_second = BETA_TWO * m2n.astype(F32) + (1.0 - BETA_TWO) * g * g
    update = new_first / (jnp.sqrt(new_second) + EPSILON)
    shape = first_moment.shape
    return (
        act.reshape(TOK, 2, FW),
        wn.reshape(weights.shape),
        new_first.reshape(shape),
        new_second.reshape(shape),
        update.reshape(shape),
    )


def solution(mesh):
    in_specs = (
        P(("expert", "replica"), None),
        P(("expert", "replica"), None),
        P(("expert", "replica"), None, None),
        P("expert", "replica", None),
        P("expert", "replica", None),
        P("expert", "replica", None),
        P(),
    )
    out_specs = (
        P(("expert", "replica"), None, None),
        P("expert", "replica", None),
        P("expert", "replica", None),
        P("expert", "replica", None),
        P("expert", "replica", None),
    )
    return jax.shard_map(body, mesh=mesh, in_specs=in_specs, out_specs=out_specs, check_vma=False)
```

time: 442 us -> 177 us (0.40)
  waiting for transfers between devices: 245 us -> 0 us
  Pallas kernels: 0 us -> 167 us
  blocking collectives: 83 us -> 0 us
  local copies, waits for them, and re-layouts: 36.1 us -> 5.61 us
  starting transfers between devices: 29.9 us -> 0 us
  matrix products: 18.1 us -> 0 us
  between operations: 14.3 us -> 0.65 us
  other arithmetic: 14.5 us -> 3.37 us
    pallas_call x0 -> x1, Pallas kernels: none -> 167 us  [body(): pl.pallas_call(kernel, out_shape=(jax.ShapeDtypeStruct((TOK, 2 * FW), BF)...]
    all_to_all x7 -> x0, waiting for transfers between devices: 138 us -> none  [the longest x1 34.7 us: relocate_state(): lax.all_to_all(first_chosen, 'expert', split_axis=0, concat_axis=0, tiled...]
    psum x1 -> x0, waiting for transfers between devices: 107 us -> none  [body(): lax.psum(partial_value.astype(jnp.bfloat16), 'replica').astype(jnp.float32)]
    all_to_all x2 -> x0, blocking collectives: 83 us -> none  [the longest x1 69.3 us: body(): lax.all_to_all(sent_rows.reshape(slot_count, capacity, model_width), 'exp...]
    all_to_all x7 -> x0, starting transfers between devices: 29.7 us -> none  [the longest x1 6.88 us: relocate_weight(): lax.all_to_all(pieces, 'expert', split_axis=0, concat_axis=0, tiled=True)]
    dot_general x2 -> x0, matrix products: 18.1 us -> none  [the longest x1 10.7 us: body(): jnp.dot(came_rows, lax.all_gather(weight_shard, 'replica', axis=0, tiled=...]
    scatter x2 -> x0, local copies, waits for them, and re-layouts: 13.8 us -> none  [the longest x1 10.9 us: body(): sent_rows = jnp.zeros((slot_count * capacity, model_width), jnp.bfloat16)...]
    gather x5 -> x0, local copies, waits for them, and re-layouts: 7.24 us -> none  [the longest x1 3.01 us: relocate_state(): first_chosen = jnp.take(first_spread, pairing, axis=0)]
  transfers between devices with their start and end apart: 9 -> 0, of which waited for: 7 -> 0; matrix products, arithmetic and copies ran while one was open for 14% -> 0% of each run, Pallas kernels for 0% -> 0%
where the time goes in v1:
time: 177 us
  Pallas kernels  167 us (94%)
  local copies, waits for them, and re-layouts  5.61 us (3%)
  other arithmetic  3.37 us (2%)
    pallas_call x1, Pallas kernels, body(): pl.pallas_call(kernel, out_shape=(jax.ShapeDtypeStruct((TOK, 2 * FW), BF)...  167 us

profile of v1, /device:TPU:1, one launch (start us, length us, event | category | flops | bytes accessed | tf_op | source)
XLA Modules:
  0.0 177.0 jit_solution(14943499796866831086)
XLA Ops:
  0.6 2.0 %copy.12 = bf16[16,8,2,1280]{3,1,2,0:T(8,128)(2,1)} copy(bf16[16,8,2,1280]{3,2,1,0:T(2,128)(2,1)} %bitcast.16) | data formatting | bytes 1310720
  2.6 167.4 %shard_map.110 = (bf16[128,2560]{1,0:T(8,128)(2,1)}, bf16[224,1280]{1,0:T(8,128)(2,1)}, bf16[224,1280]{1,0:T(8,128)(2,1)}, bf16[224,1280]{1,0:T(8,128)(2,1)}, f32[224,1280]{1,0:T(8,128)}) custom-call(s32[8]{0:T(128)} %pair.1, s32[2,128]{1,0:T(2,128)} %bitcast.19, bf16[128,3584]{1,0:T(8,128)(2,1)} %tok.1, bf16[128,2560]{1,0:T(8,128)(2,1)} %bitcast.13, ...), custom_call_target="tpu_custom_call" | custom-call | tf_op jit(solution)/shard_map/pallas_call | solution.py:423
  170.0 0.0 copy-start
  170.0 2.8 %reshape.41 = bf16[128,2,1280]{2,1,0:T(2,128)(2,1)} reshape(bf16[128,2560]{1,0:T(8,128)(2,1)} %get-tuple-element.10) | data formatting | bytes 1310720 | tf_op jit(solution)/shard_map/reshape | solution.py:482
  172.8 0.0 copy-done
  172.8 0.0 copy-start.1
  172.8 3.4 %divide_bitcast_fusion = (f32[1,224,1280]{2,1,0:T(8,128)}, f32[1,224,1280]{2,1,0:T(8,128)}, f32[1,224,1280]{2,1,0:T(8,128)}) fusion(f32[224,1280]{1,0:T(8,128)S(1)} %copy-done, bf16[224,1280]{1,0:T(8,128)(2,1)} %get-tuple-element.12, bf16[224,1280]{1,0:T(8,128)(2,1)} %get-tuple-element.14), kind=kLoop, calls=%fused_computation.2 | loop fusion | flops 3153920 | bytes 5734400 | tf_op jit(solution)/shard_map/reshape | solution.py:486
  176.2 0.0 copy-done.1
  176.2 0.8 copy.14
Async XLA Ops:
  170.0 2.8 %copy-start = (f32[224,1280]{1,0:T(8,128)S(1)}, f32[224,1280]{1,0:T(8,128)}, u32[]{:S(2)}) copy-start(f32[224,1280]{1,0:T(8,128)} %get-tuple-element.13) | copy-start | bytes 3440644
  172.8 3.4 %copy-start.1 = (bf16[224,1280]{1,0:T(8,128)(2,1)S(1)}, bf16[224,1280]{1,0:T(8,128)(2,1)}, u32[]{:S(2)}) copy-start(bf16[224,1280]{1,0:T(8,128)(2,1)} %get-tuple-element.11) | copy-start | bytes 1720324

commit v2 on v1

v2 whole, which is shorter than its diff:
```python
import jax
import jax.numpy as jnp
from jax import lax
from jax.experimental import pallas as pl
from jax.experimental.pallas import tpu as pltpu
from jax.sharding import PartitionSpec as P

BETA_ONE = 0.8
BETA_TWO = 0.9
EPSILON = 1e-08
MESH = pl.DeviceIdType.MESH
BF = jnp.bfloat16
F32 = jnp.float32

D, FW, TOK, CAP, NE, SHARD, CHUNK = 3584, 1280, 128, 64, 8, 224, 896
ROWS = NE * CAP
TILE = 256
WIDE = 640
HALF = 112


def kernel(
    pair, rt, tok, cot, w, m1, m2,
    act, wn, m1n, m2n, g,
    w1, w2s, wfull, b1s, b1r, b2s, b2r, tp, tr, cp, cr, acc, ps, pr, part, sibr, xr, yr, g0, g1,
    rnb, tnb, cnb, near, far_,
    s_m, s_w1, r_w1, s_w2, r_w2, s_b1, r_b1, s_b2, r_b2, s_t, r_t, s_c, r_c, s_e, r_e,
    s_ag, r_ag, s_sb, r_sb, s_x, r_x, s_y, r_y, s_nb, r_nb,
):
    e = lax.axis_index("expert")
    r = lax.axis_index("replica")
    x = r // 4
    yh = (r // 2) % 2
    c = r % 2

    def rid(x_, yh_, c_):
        return x_ * 4 + yh_ * 2 + c_

    xp, xm, xo = (x + 1) % 4, (x + 3) % 4, (x + 2) % 4
    z, yl = e // 2, e % 2
    ne = e + 1 - 2 * yl
    nb = (ne, r)
    order = (xo, xp, xm, x)
    sib = (e, rid(x, yh, 1 - c))
    yp = (e, rid(x, 1 - yh, c))
    px = (e, rid(xp, yh, c))
    mx = (e, rid(xm, yh, c))

    def rc(src, dst, ss, rs, dev):
        return pltpu.make_async_remote_copy(
            src_ref=src, dst_ref=dst, send_sem=ss, recv_sem=rs, device_id=dev, device_id_type=MESH
        )

    def got(ref, sem):
        rc(ref, ref, sem, sem, sib).wait_recv()

    def gone(ref, sem):
        rc(ref, ref, sem, sem, sib).wait_send()

    loads = [
        pltpu.make_async_copy(m1, acc.at[pl.ds(0, SHARD)], s_m.at[0]),
        pltpu.make_async_copy(m2, acc.at[pl.ds(SHARD, SHARD)], s_m.at[1]),
    ]
    for load in loads:
        load.start()

    barrier = pltpu.get_barrier_semaphore()

    @pl.loop(1, NE)
    def _(d):
        pl.semaphore_signal(barrier, inc=1, device_id=((e + d) % NE, r), device_id_type=MESH)

    for dev in (sib, yp, px, mx):
        pl.semaphore_signal(barrier, inc=1, device_id=dev, device_id_type=MESH)
    pl.semaphore_wait(barrier, NE - 1 + 4)

    def raw(k):
        cols = pl.ds(pl.multiple_of(order[k] * CHUNK, 128), CHUNK)
        return rc(tok.at[:, cols], tnb.at[k], s_nb.at[k], r_nb.at[k], nb)

    raw_routes = rc(rt, rnb, s_nb.at[4], r_nb.at[4], nb)
    raw_cot = rc(cot, cnb, s_nb.at[5], r_nb.at[5], nb)
    raw_routes.start()

    @pl.loop(0, 7)
    def _(i):
        rows = pl.ds(pl.multiple_of(i * 32, 32), 32)

        @pl.when(i != e)
        def _():
            rc(w.at[rows], w1.at[e], s_w1.at[i], r_w1.at[e], (i, r)).start()

        @pl.when(i == e)
        def _():
            w1[e] = w[rows, :]

    raw(0).start()

    places = lax.broadcasted_iota(jnp.int32, (NE, TOK), 0)
    earlier = jnp.where(
        lax.broadcasted_iota(jnp.int32, (TOK, TOK), 0) < lax.broadcasted_iota(jnp.int32, (TOK, TOK), 1), 1.0, 0.0
    ).astype(BF)

    def placed(ref):
        owners = []
        for k in range(2):
            row = ref[k : k + 1, :]
            own = jnp.zeros_like(row)
            for s in range(NE):
                own = own + jnp.where(row == s, pair[s], 0)
            owners.append(own)
        named = [(places == own) for own in owners]
        mask = jnp.where(named[0] | named[1], 1.0, 0.0).astype(BF)
        rank = jnp.dot(mask, earlier, preferred_element_type=F32)
        ranks = [jnp.sum(jnp.where(one, rank, 0.0), axis=0, keepdims=True) for one in named]
        return owners, ranks

    def one_hot(slot, ref, rows):
        slots = lax.broadcasted_iota(jnp.int32, (rows, TOK), 0).astype(F32)
        ref[...] = jnp.where(slots == slot, 1.0, 0.0).astype(BF)

    def along_z(owners, ranks, ref):
        for k in range(2):
            slot = (owners[k] >> 1).astype(F32) * CAP + ranks[k]
            one_hot(jnp.where((owners[k] & 1) == yl, slot, -1.0), ref.at[k], NE * CAP // 2)

    owners, ranks = placed(rt)
    along_z(owners, ranks, near)

    def to_z(src, dst, ss, rs):
        @pl.loop(1, 4)
        def _(d):
            t = (z + d) % 4
            rc(src(t), dst, ss(t), rs, (t * 2 + yl, r)).start()

    def send_cot(half):
        hot, src, owner = ((near, cot, e), (far_, cnb, ne))[half]

        @pl.loop(0, FW // TILE)
        def _(n):
            cols = pl.ds(pl.multiple_of(n * TILE, TILE), TILE)
            a = jnp.dot(hot[0], src[:, 0, cols], preferred_element_type=F32)
            b = jnp.dot(hot[1], src[:, 1, cols], preferred_element_type=F32)
            cp[half, :, :, cols] = (a + b).astype(BF).reshape(4, CAP, TILE)

        to_z(lambda t: cp.at[half, t], cr.at[owner], lambda t: s_c.at[half, t], r_c.at[owner])
        cr[owner] = cp[half, z]

    def send_tok(half, k):
        hot, owner = ((near, e), (far_, ne))[half]
        q = order[k]
        src = tok[:, pl.ds(pl.multiple_of(q * CHUNK, 128), CHUNK)] if half == 0 else tnb[k]
        v = jnp.dot(hot[0] + hot[1], src, preferred_element_type=F32)
        tp[k, half] = v.astype(BF).reshape(4, CAP, CHUNK)
        to_z(lambda t: tp.at[k, half, t], tr.at[q, owner], lambda t: s_t.at[k, half, t], r_t.at[k, owner])
        tr[q, owner] = tp[k, half, z]

    send_cot(0)

    @pl.when(e < 7)
    def _():
        @pl.loop(0, NE)
        def _(s):
            @pl.when(s != e)
            def _():
                got(w1.at[s], r_w1.at[s])

        rows = pl.ds(pl.multiple_of(e * 32, 32), 32)

        @pl.loop(0, NE)
        def _(s):
            v = w1[pair[s]]
            w2s[s] = v

            @pl.when(s != e)
            def _():
                rc(w2s.at[s], wfull.at[r, rows], s_w2.at[s], r_w2.at[e], (s, r)).start()

            @pl.when(s == e)
            def _():
                wfull[r, rows, :] = v

    send_tok(0, 0)
    send_tok(0, 1)
    raw_routes.wait_recv()
    along_z(*placed(rnb), far_)
    for k in range(2):
        one_hot(owners[k].astype(F32) * CAP + ranks[k], (g0, g1)[k], ROWS)

    @pl.loop(0, 7)
    def _(i):
        @pl.when(i != e)
        def _():
            got(wfull.at[r, pl.ds(pl.multiple_of(i * 32, 32), 32)], r_w2.at[i])

    def ag(shard, k, dev):
        rc(wfull.at[shard], wfull.at[shard], s_ag.at[k], r_ag.at[shard], dev).start()

    ag(r, 0, yp)
    ag(r, 1, px)
    ag(r, 2, mx)
    ag(r, 3, sib)

    raw_cot.start()
    for k in range(1, 4):
        raw(k).start()
    send_tok(0, 2)
    send_tok(0, 3)
    raw(0).wait_recv()
    send_tok(1, 0)
    wn[...] = wfull[r]

    def from_x(h, k):
        low, high = rid(xm, h, c), rid(xp, h, c)
        got(wfull.at[low], r_ag.at[low])
        ag(low, k, sib)
        got(wfull.at[high], r_ag.at[high])
        ag(high, k + 1, sib)
        ag(rid((x + 3 + 2 * h) % 4, h, c), k + 2, (e, rid((x + 1 + 2 * h) % 4, yh, c)))

    partner = rid(x, 1 - yh, c)
    got(wfull.at[partner], r_ag.at[partner])
    ag(partner, 4, px)
    ag(partner, 5, mx)
    ag(partner, 6, sib)
    from_x(yh, 7)

    def other_z(take):
        @pl.loop(1, 4)
        def _(d):
            t = (z + d) % 4
            take(t * 2 + yl)
            take(t * 2 + 1 - yl)

    def wgrad(k):
        q = order[k]
        other_z(lambda s: got(tr.at[q, s], r_t.at[k, s]))

        @pl.loop(0, FW // WIDE)
        def _(n):
            cols = pl.ds(pl.multiple_of(n * WIDE, WIDE), WIDE)
            v = lax.dot_general(
                tr[q].reshape(ROWS, CHUNK), cr[:, :, cols].reshape(ROWS, WIDE), (((0,), (0,)), ((), ())),
                preferred_element_type=F32,
            )
            part[pl.ds(q * 4, 4), :, cols] = v.astype(BF).reshape(4, SHARD, WIDE)

    def add(shard, other, half):
        @pl.loop(0, 7)
        def _(i):
            rows = pl.ds(pl.multiple_of(half * HALF + i * 16, 16), 16)
            part[shard, rows, :] = (part[shard, rows, :].astype(F32) + other[rows, :].astype(F32)).astype(BF)

    def to_sib(k):
        for h in range(2):
            rc(
                part.at[rid(order[k], h, 1 - c)], sibr.at[2 * k + h], s_sb.at[2 * k + h], r_sb.at[2 * k + h], sib
            ).start()

    def xs(h, k, slot, half, dev):
        rows = pl.ds(half * HALF, HALF)
        rc(
            part.at[rid(order[k], h, c), rows], xr.at[slot, rows], s_x.at[slot, half], r_x.at[slot, half], dev
        ).start()

    def with_sib(k, h, slot=None, dev=None):
        got(sibr.at[2 * k + h], r_sb.at[2 * k + h])
        for half in range(2):
            add(rid(order[k], h, c), sibr.at[2 * k + h], half)
            if dev is not None:
                xs(h, k, slot, half, dev)

    def with_x(k, h, came, slot, dev):
        for half in range(2):
            got(xr.at[came, pl.ds(half * HALF, HALF)], r_x.at[came, half])
            add(rid(order[k], h, c), xr.at[came], half)
            xs(h, k, slot, half, dev)

    def project(q, first):
        @pl.loop(0, FW // WIDE)
        def _(n):
            cols = pl.ds(pl.multiple_of(n * WIDE, WIDE), WIDE)
            v = jnp.dot(
                tr[q].reshape(ROWS, CHUNK), wfull[pl.ds(q * 4, 4), :, cols].reshape(CHUNK, WIDE),
                preferred_element_type=F32,
            )
            if first:
                acc[:, cols] = v
            else:
                acc[:, cols] += v

    def sib_has(q):
        for h in range(2):
            shard = rid(q, h, 1 - c)
            got(wfull.at[shard], r_ag.at[shard])


    raw_cot.wait_recv()
    send_cot(1)
    raw(1).wait_recv()
    send_tok(1, 1)
    from_x(1 - yh, 10)

    other_z(lambda s: got(cr.at[s], r_c.at[s]))
    wgrad(0)
    to_sib(0)
    raw(2).wait_recv()
    send_tok(1, 2)
    with_sib(0, 0, 0, px)
    with_sib(0, 1, 1, mx)
    raw(3).wait_recv()
    send_tok(1, 3)

    for load in loads:
        load.wait()

    @pl.loop(0, NE)
    def _(p):
        rows = pl.ds(pl.multiple_of((p // 4) * SHARD + ((p // 2) % 2) * 112, 8), 112)
        cols = pl.ds(pl.multiple_of((p % 2) * 640, 128), 640)
        b1s[p] = acc[rows, cols].astype(BF)

        @pl.when(p != e)
        def _():
            rc(b1s.at[p], b1r.at[e], s_b1.at[p], r_b1.at[e], (p, r)).start()

        @pl.when(p == e)
        def _():
            b1r[e] = b1s[p]

    wgrad(1)
    to_sib(1)
    far = (rid(xo, yh, c), rid(xo, 1 - yh, c))
    for k in range(2):
        got(wfull.at[far[k]], r_ag.at[far[k]])
        ag(far[k], 13 + k, sib)
    with_sib(1, 1, 3, px)
    with_sib(1, 0)
    wgrad(2)
    to_sib(2)
    sib_has(xo)
    project(xo, True)
    with_sib(2, 0, 5, mx)
    with_sib(2, 1)
    wgrad(3)
    to_sib(3)
    sib_has(xp)
    project(xp, False)
    sib_has(xm)
    project(xm, False)
    sib_has(x)
    project(x, False)

    @pl.loop(0, NE)
    def _(s):
        ps[s] = acc[pl.ds(pl.multiple_of(s * CAP, CAP), CAP), :].astype(BF)

        @pl.when(s != e)
        def _():
            rc(ps.at[s], pr.at[e], s_e.at[s], r_e.at[e], (s, r)).start()

        @pl.when(s == e)
        def _():
            pr[e] = ps[s]

    with_x(1, 0, 0, 2, px)
    with_x(2, 1, 1, 4, mx)
    with_sib(3, 0)
    with_sib(3, 1)

    @pl.loop(1, NE)
    def _(d):
        s = (e + d) % NE
        got(b1r.at[s], r_b1.at[s])

    @pl.loop(0, NE)
    def _(s):
        v = b1r[pair[s]]
        b2s[s] = v

        @pl.when(s != e)
        def _():
            rc(b2s.at[s], b2r.at[e], s_b2.at[s], r_b2.at[e], (s, r)).start()

        @pl.when(s == e)
        def _():
            b2r[e] = v

    def total(h, half, put):
        @pl.loop(0, 7)
        def _(i):
            rows = pl.ds(pl.multiple_of(half * HALF + i * 16, 16), 16)
            put(
                rows,
                part[rid(x, h, c), rows, :].astype(F32)
                + xr[2 + h, rows, :].astype(F32)
                + xr[5 - h, rows, :].astype(F32),
            )

    def put_part(rows, v):
        part[partner, rows, :] = v.astype(BF)

    def put_g(rows, v):
        g[rows, :] = v

    def ysend(half):
        rows = pl.ds(half * HALF, HALF)
        return rc(part.at[partner, rows], yr.at[rows], s_y.at[half], r_y.at[half], yp)

    for half in range(2):
        for k in range(2, 6):
            got(xr.at[k, pl.ds(half * HALF, HALF)], r_x.at[k, half])
        total(1 - yh, half, put_part)
        ysend(half).start()
        total(yh, half, put_g)

    @pl.loop(1, NE)
    def _(d):
        s = (e + d) % NE
        got(b2r.at[s], r_b2.at[s])

    for i in range(NE):
        out = m1n if i < 4 else m2n
        a, b = (i // 2) % 2, i % 2
        out[112 * a : 112 * a + 112, 640 * b : 640 * b + 640] = b2r[i]

    @pl.loop(1, NE)
    def _(d):
        s = (e + d) % NE
        got(pr.at[s], r_e.at[s])

    @pl.loop(0, FW // TILE)
    def _(n):
        cols = pl.ds(pl.multiple_of(n * TILE, TILE), TILE)
        for k, ref in ((0, g0), (1, g1)):
            v = lax.dot_general(
                ref[...], pr[:, :, cols].reshape(ROWS, TILE), (((0,), (0,)), ((), ())), preferred_element_type=F32
            )
            act[:, k, cols] = v.astype(BF)

    for half in range(2):
        ysend(half).wait_recv()

        @pl.loop(0, 7)
        def _(i):
            rows = pl.ds(pl.multiple_of(half * HALF + i * 16, 16), 16)
            g[rows, :] += yr[rows, :].astype(F32)

    for half in range(2):
        ysend(half).wait_send()
    for k in range(15):
        gone(wfull.at[0], s_ag.at[k])

    @pl.loop(0, 7)
    def _(i):
        @pl.when(i != e)
        def _():
            gone(w1.at[0], s_w1.at[i])

    @pl.loop(0, NE)
    def _(s):
        gone(sibr.at[0], s_sb.at[s])

    @pl.loop(0, 6)
    def _(s):
        for half in range(2):
            gone(xr.at[0, pl.ds(0, HALF)], s_x.at[s, half])

    @pl.loop(1, NE)
    def _(d):
        s = (e + d) % NE

        @pl.when(e < 7)
        def _():
            gone(w2s.at[0], s_w2.at[s])

        gone(b1s.at[0], s_b1.at[s])
        gone(b2s.at[0], s_b2.at[s])
        gone(ps.at[0], s_e.at[s])

    @pl.loop(1, 4)
    def _(d):
        t = (z + d) % 4
        for half in range(2):
            gone(cp.at[0, 0], s_c.at[half, t])
            for k in range(4):
                gone(tp.at[0, 0, 0], s_t.at[k, half, t])

    raw_routes.wait_send()
    raw_cot.wait_send()
    for k in range(4):
        raw(k).wait_send()


def body(tokens, routes, cotangent, weights, first_moment, second_moment, pairing):
    dma = pltpu.SemaphoreType.DMA
    vmem = pl.BlockSpec(memory_space=pltpu.VMEM)
    hbm = pl.BlockSpec(memory_space=pl.ANY)
    act, wn, m1n, m2n, g = pl.pallas_call(
        kernel,
        out_shape=(
            jax.ShapeDtypeStruct((TOK, 2, FW), BF),
            jax.ShapeDtypeStruct((SHARD, FW), BF),
            jax.ShapeDtypeStruct((SHARD, FW), BF),
            jax.ShapeDtypeStruct((SHARD, FW), BF),
            jax.ShapeDtypeStruct((SHARD, FW), F32),
        ),
        in_specs=[pl.BlockSpec(memory_space=pltpu.SMEM), vmem, vmem, vmem, vmem, hbm, hbm],
        out_specs=(vmem,) * 5,
        scratch_shapes=[
            pltpu.VMEM((NE, 32, FW), BF),
            pltpu.VMEM((NE, 32, FW), BF),
            pltpu.VMEM((16, SHARD, FW), BF),
            pltpu.VMEM((NE, 112, 640), BF),
            pltpu.VMEM((NE, 112, 640), BF),
            pltpu.VMEM((NE, 112, 640), BF),
            pltpu.VMEM((NE, 112, 640), BF),
            pltpu.VMEM((4, 2, 4, CAP, CHUNK), BF),
            pltpu.VMEM((4, NE, CAP, CHUNK), BF),
            pltpu.VMEM((2, 4, CAP, FW), BF),
            pltpu.VMEM((NE, CAP, FW), BF),
            pltpu.VMEM((ROWS, FW), F32),
            pltpu.VMEM((NE, CAP, FW), BF),
            pltpu.VMEM((NE, CAP, FW), BF),
            pltpu.VMEM((16, SHARD, FW), BF),
            pltpu.VMEM((NE, SHARD, FW), BF),
            pltpu.VMEM((6, SHARD, FW), BF),
            pltpu.VMEM((SHARD, FW), BF),
            pltpu.VMEM((ROWS, TOK), BF),
            pltpu.VMEM((ROWS, TOK), BF),
            pltpu.VMEM((2, TOK), jnp.int32),
            pltpu.VMEM((4, TOK, CHUNK), BF),
            pltpu.VMEM((TOK, 2, FW), BF),
            pltpu.VMEM((2, ROWS // 2, TOK), BF),
            pltpu.VMEM((2, ROWS // 2, TOK), BF),
            dma((2,)),
            dma((NE,)), dma((NE,)), dma((NE,)), dma((NE,)),
            dma((NE,)), dma((NE,)), dma((NE,)), dma((NE,)),
            dma((4, 2, 4)), dma((4, NE)),
            dma((2, 4)), dma((NE,)), dma((NE,)), dma((NE,)),
            dma((15,)), dma((16,)),
            dma((NE,)), dma((NE,)),
            dma((6, 2)), dma((6, 2)),
            dma((2,)), dma((2,)),
            dma((6,)), dma((6,)),
        ],
        compiler_params=pltpu.CompilerParams(
            collective_id=0, has_side_effects=True, vmem_limit_bytes=63 * 1024 * 1024
        ),
    )(
        pairing,
        routes.T,
        tokens,
        cotangent,
        weights.reshape(SHARD, FW),
        first_moment.reshape(SHARD, FW),
        second_moment.reshape(SHARD, FW),
    )
    new_first = BETA_ONE * m1n.astype(F32) + (1.0 - BETA_ONE) * g
    new_second = BETA_TWO * m2n.astype(F32) + (1.0 - BETA_TWO) * g * g
    update = new_first / (jnp.sqrt(new_second) + EPSILON)
    shape = first_moment.shape
    return (
        act,
        wn.reshape(weights.shape),
        new_first.reshape(shape),
        new_second.reshape(shape),
        update.reshape(shape),
    )


def solution(mesh):
    in_specs = (
        P(("expert", "replica"), None),
        P(("expert", "replica"), None),
        P(("expert", "replica"), None, None),
        P("expert", "replica", None),
        P("expert", "replica", None),
        P("expert", "replica", None),
        P(),
    )
    out_specs = (
        P(("expert", "replica"), None, None),
        P("expert", "replica", None),
        P("expert", "replica", None),
        P("expert", "replica", None),
        P("expert", "replica", None),
    )
    return jax.shard_map(body, mesh=mesh, in_specs=in_specs, out_specs=out_specs, check_vma=False)
```

time: 177 us -> 157 us (0.89)
  Pallas kernels: 167 us -> 151 us
  local copies, waits for them, and re-layouts: 5.61 us -> 2.11 us
    pallas_call x1, Pallas kernels: 167 us -> 151 us  [body(): pl.pallas_call(kernel, out_shape=(jax.ShapeDtypeStruct((TOK, 2, FW), BF),...]
    reshape x1 -> x0, local copies, waits for them, and re-layouts: 2.8 us -> none  [body(): act.reshape(TOK, 2, FW)]
where the time goes in v2:
time: 157 us
  Pallas kernels  151 us (96%)
  other arithmetic  3.72 us (2%)
  local copies, waits for them, and re-layouts  2.11 us (1%)
    pallas_call x1, Pallas kernels, body(): pl.pallas_call(kernel, out_shape=(jax.ShapeDtypeStruct((TOK, 2, FW), BF),...  151 us
    reshape x1, other arithmetic, body(): update.reshape(shape)  3.72 us

profile of v2, /device:TPU:1, one launch (start us, length us, event | category | flops | bytes accessed | tf_op | source)
XLA Modules:
  0.0 157.2 jit_solution(9883369493973508271)
XLA Ops:
  0.6 150.7 %shard_map.110 = (bf16[128,2,1280]{2,1,0:T(2,128)(2,1)}, bf16[224,1280]{1,0:T(8,128)(2,1)}, bf16[224,1280]{1,0:T(8,128)(2,1)}, bf16[224,1280]{1,0:T(8,128)(2,1)}, f32[224,1280]{1,0:T(8,128)}) custom-call(s32[8]{0:T(128)} %pair.1, s32[2,128]{1,0:T(2,128)} %bitcast.15, bf16[128,3584]{1,0:T(8,128)(2,1)} %tok.1, bf16[128,2,1280]{2,1,0:T(2,128)(2,1)} %cot.1, ...), custom_call_target="tpu_custom_call" | custom-call | tf_op jit(solution)/shard_map/pallas_call | solution.py:499
  151.4 0.0 copy-start
  151.4 3.7 %divide_bitcast_fusion = (f32[1,224,1280]{2,1,0:T(8,128)}, f32[1,224,1280]{2,1,0:T(8,128)}, f32[1,224,1280]{2,1,0:T(8,128)}) fusion(f32[224,1280]{1,0:T(8,128)} %get-tuple-element.13, bf16[224,1280]{1,0:T(8,128)(2,1)} %get-tuple-element.12, bf16[224,1280]{1,0:T(8,128)(2,1)} %get-tuple-element.14), kind=kLoop, calls=%fused_computation.2 | loop fusion | flops 3153920 | bytes 5734400 | tf_op jit(solution)/shard_map/reshape | solution.py:568
  155.1 0.0 copy-start.1
  155.1 0.0 copy-done
  155.1 0.8 copy.14
  156.0 0.5 copy-done.1
  156.4 0.8 copy.15
Async XLA Ops:
  151.4 3.7 %copy-start = (bf16[128,2,1280]{2,1,0:T(2,128)(2,1)S(1)}, bf16[128,2,1280]{2,1,0:T(2,128)(2,1)}, u32[]{:S(2)}) copy-start(bf16[128,2,1280]{2,1,0:T(2,128)(2,1)} %get-tuple-element.23) | copy-start | bytes 1966084
  155.1 1.3 copy-start.1

commit v3 on v2

--- a/solution.py
+++ b/solution.py
@@ -82,17 +82,18 @@
     raw_cot = rc(cot, cnb, s_nb.at[5], r_nb.at[5], nb)
     raw_routes.start()
 
-    @pl.loop(0, 7)
-    def _(i):
-        rows = pl.ds(pl.multiple_of(i * 32, 32), 32)
-
-        @pl.when(i != e)
-        def _():
+    @pl.loop(1, NE)
+    def _(d):
+        i = (e + d) % NE
+
+        @pl.when(i < 7)
+        def _():
+            rows = pl.ds(pl.multiple_of(i * 32, 32), 32)
             rc(w.at[rows], w1.at[e], s_w1.at[i], r_w1.at[e], (i, r)).start()
 
-        @pl.when(i == e)
-        def _():
-            w1[e] = w[rows, :]
+    @pl.when(e < 7)
+    def _():
+        w1[e] = w[pl.ds(pl.multiple_of(e * 32, 32), 32), :]
 
     raw(0).start()
 
@@ -167,8 +168,9 @@
 
         rows = pl.ds(pl.multiple_of(e * 32, 32), 32)
 
-        @pl.loop(0, NE)
-        def _(s):
+        @pl.loop(1, NE + 1)
+        def _(d):
+            s = (e + d) % NE
             v = w1[pair[s]]
             w2s[s] = v
 
@@ -297,9 +299,9 @@
 
     raw_cot.wait_recv()
     send_cot(1)
+    from_x(1 - yh, 10)
     raw(1).wait_recv()
     send_tok(1, 1)
-    from_x(1 - yh, 10)
 
     other_z(lambda s: got(cr.at[s], r_c.at[s]))
     wgrad(0)
@@ -314,8 +316,9 @@
     for load in loads:
         load.wait()
 
-    @pl.loop(0, NE)
-    def _(p):
+    @pl.loop(1, NE + 1)
+    def _(d):
+        p = (e + d) % NE
         rows = pl.ds(pl.multiple_of((p // 4) * SHARD + ((p // 2) % 2) * 112, 8), 112)
         cols = pl.ds(pl.multiple_of((p % 2) * 640, 128), 640)
         b1s[p] = acc[rows, cols].astype(BF)
@@ -336,23 +339,24 @@
         ag(far[k], 13 + k, sib)
     with_sib(1, 1, 3, px)
     with_sib(1, 0)
+    sib_has(xp)
+    project(xp, True)
     wgrad(2)
     to_sib(2)
-    sib_has(xo)
-    project(xo, True)
     with_sib(2, 0, 5, mx)
     with_sib(2, 1)
+    sib_has(xm)
+    project(xm, False)
+    sib_has(xo)
+    project(xo, False)
     wgrad(3)
     to_sib(3)
-    sib_has(xp)
-    project(xp, False)
-    sib_has(xm)
-    project(xm, False)
     sib_has(x)
     project(x, False)
 
-    @pl.loop(0, NE)
-    def _(s):
+    @pl.loop(1, NE + 1)
+    def _(d):
+        s = (e + d) % NE
         ps[s] = acc[pl.ds(pl.multiple_of(s * CAP, CAP), CAP), :].astype(BF)
 
         @pl.when(s != e)
@@ -373,8 +377,9 @@
         s = (e + d) % NE
         got(b1r.at[s], r_b1.at[s])
 
-    @pl.loop(0, NE)
-    def _(s):
+    @pl.loop(1, NE + 1)
+    def _(d):
+        s = (e + d) % NE
         v = b1r[pair[s]]
         b2s[s] = v
 

time: 157 us -> 150 us (0.955); the launches traced: 157 us -> 148 us
  Pallas kernels: 151 us -> 142 us
    pallas_call x1, Pallas kernels: 151 us -> 142 us  [body(): pl.pallas_call(kernel, out_shape=(jax.ShapeDtypeStruct((TOK, 2, FW), BF),...]
where the time goes in v3:
time: 150 us; the launch traced here: 148 us
  Pallas kernels  142 us (95%)
  other arithmetic  3.72 us (2%)
  local copies, waits for them, and re-layouts  2.11 us (1%)
    pallas_call x1, Pallas kernels, body(): pl.pallas_call(kernel, out_shape=(jax.ShapeDtypeStruct((TOK, 2, FW), BF),...  142 us
    reshape x1, other arithmetic, body(): update.reshape(shape)  3.72 us

profile of v3, /device:TPU:1, one launch (start us, length us, event | category | flops | bytes accessed | tf_op | source)
XLA Modules:
  0.0 148.0 jit_solution(2580861877220621077)
XLA Ops:
  0.6 141.6 %shard_map.110 = (bf16[128,2,1280]{2,1,0:T(2,128)(2,1)}, bf16[224,1280]{1,0:T(8,128)(2,1)}, bf16[224,1280]{1,0:T(8,128)(2,1)}, bf16[224,1280]{1,0:T(8,128)(2,1)}, f32[224,1280]{1,0:T(8,128)}) custom-call(s32[8]{0:T(128)} %pair.1, s32[2,128]{1,0:T(2,128)} %bitcast.15, bf16[128,3584]{1,0:T(8,128)(2,1)} %tok.1, bf16[128,2,1280]{2,1,0:T(2,128)(2,1)} %cot.1, ...), custom_call_target="tpu_custom_call" | custom-call | tf_op jit(solution)/shard_map/pallas_call | solution.py:504
  142.2 0.0 copy-start
  142.2 3.7 %divide_bitcast_fusion = (f32[1,224,1280]{2,1,0:T(8,128)}, f32[1,224,1280]{2,1,0:T(8,128)}, f32[1,224,1280]{2,1,0:T(8,128)}) fusion(f32[224,1280]{1,0:T(8,128)} %get-tuple-element.13, bf16[224,1280]{1,0:T(8,128)(2,1)} %get-tuple-element.12, bf16[224,1280]{1,0:T(8,128)(2,1)} %get-tuple-element.14), kind=kLoop, calls=%fused_computation.2 | loop fusion | flops 3153920 | bytes 5734400 | tf_op jit(solution)/shard_map/reshape | solution.py:573
  145.9 0.0 copy-start.1
  145.9 0.0 copy-done
  145.9 0.8 copy.14
  146.8 0.5 copy-done.1
  147.2 0.8 copy.15
Async XLA Ops:
  142.2 3.7 %copy-start = (bf16[128,2,1280]{2,1,0:T(2,128)(2,1)S(1)}, bf16[128,2,1280]{2,1,0:T(2,128)(2,1)}, u32[]{:S(2)}) copy-start(bf16[128,2,1280]{2,1,0:T(2,128)(2,1)} %get-tuple-element.23) | copy-start | bytes 1966084
  145.9 1.3 copy-start.1
